TPU v7x, 256 devices: a whole 4x4x8 slice. The times are simulated.
256 devices in a mesh: fsdp: 16 (over x_lo, y, core), group: 8 (over z), dp: 2 (over x_hi).
Axes of the slice: x: 4 (x_hi: 2, x_lo: 2; x = x_hi * 2 + x_lo), y: 4, z: 8, core: 2. Of those that a mesh axis runs over, the one named last changes fastest.
Arguments:
- hidden_states: bfloat16 [32, 16, 256, 5120], P(('fsdp', 'dp'), 'group'), may hold values from -6 to 6
- kv_weight: bfloat16 [5120, 1024], P('fsdp'), may hold values from -0.078125 to 0.078125
- sensitivity: bfloat16 [32, 16, 256, 1024], P(('fsdp', 'dp'), 'group'), may hold values from -6 to 6
- logp_shift: float32 [32, 16, 256], P(('fsdp', 'dp'), 'group'), may hold values from -0.6 to 0.6
- token_mask: int32 [32, 16, 256], P(('fsdp', 'dp'), 'group'), may hold values 0 or 1
- lengths: int32 [32, 16], P(('fsdp', 'dp'), 'group'), may hold values from 64 to 256
- rewards: int32 [32, 16], P(('fsdp', 'dp'), 'group'), may hold values from 0 to 100
Outputs:
- kv_grad: float32 [5120, 1024], P('fsdp', 'group')
All inputs are finite; a program needn't handle non-finite values. No bound on the sum of `token_mask` on one device may be relied on, other than what follows from the above.
Results may differ from a plain program's by a relative error of at most 0.0029.
Values may be sent and summed in bfloat16 or wider, within the bound.
No kernel may reach another device: no remote copies, remote signals or barrier semaphores. Data moves between devices by JAX's collectives and lax.ppermute only.
A program may use at most 128 MiB of HBM per device.

v0:
```python
import functools
import math

import jax
import jax.numpy as jnp
from jax import lax
from jax.experimental import pallas as pl
from jax.experimental.pallas import tpu as pltpu
from jax.sharding import PartitionSpec as P

GROUP_SIZE = 16
CLIP_LOW = 0.8
CLIP_HIGH = 1.28
LOSS_SCALE = 64.0
VMEM_GRANT = 16 * 2**20

NX, NY, NC, NZ, NDP = 2, 4, 2, 8, 2
PLANE = [(x, y, c) for x in range(NX) for y in range(NY) for c in range(NC)]


def place(x, y, c):
    return (x * NY + y % NY) * NC + c


def ring_x(x, y, c, dp, hop):
    ring = (dp * NX + x + hop) % (NX * NDP)
    return place(ring % NX, y, c) * NDP + ring // NX


OTHER_CORE = [(place(x, y, c), place(x, y, 1 - c)) for x, y, c in PLANE]


def to_core(a):
    return lax.ppermute(a, "fsdp", OTHER_CORE)


def along_y(a, way):
    pairs = [(place(x, y, c), place(x, y + (way if c == 0 else -way), c)) for x, y, c in PLANE]
    return lax.ppermute(a, "fsdp", pairs)


def rows_along_y(a, way):
    pairs = []
    for x, y, c in PLANE:
        for z in range(NZ):
            owner = (c + z) % NC
            far_y = y + (1 if c == 0 else -1)
            ends = place(x, y, c) * NZ + z, place(x, far_y, owner) * NZ + z
            pairs.append(ends if way > 0 else ends[::-1])
    return lax.ppermute(a, ("fsdp", "group"), pairs)


def along_z(a):
    pairs = []
    for x, y, c in PLANE:
        for z in range(NZ):
            to = z ^ 1 if c == 0 else (z + (1 if z % 2 else -1)) % NZ
            pairs.append((place(x, y, c) * NZ + z, place(x, y, c) * NZ + to))
    return lax.ppermute(a, ("fsdp", "group"), pairs)


def along_x(a, way):
    pairs = [
        (place(x, y, c) * NDP + dp, ring_x(x, y, c, dp, way if c == 0 else -way))
        for x, y, c in PLANE
        for dp in range(NDP)
    ]
    return lax.ppermute(a, ("fsdp", "dp"), pairs)


def to_z_xor(a, bit):
    return lax.ppermute(a, "group", [(z, z ^ bit) for z in range(NZ)])


def to_dp(a):
    return lax.ppermute(a, "dp", [(0, 1), (1, 0)])


def after(a, earlier):
    return lax.optimization_barrier((a, earlier))[0]


def after(a, earlier):
    return lax.optimization_barrier((a, earlier))[0]


def owner_of(kind):
    core = lax.axis_index("fsdp") % NC
    if kind == "core":
        return core
    planar = (core + lax.axis_index("group")) % NC
    return planar if kind == "plane" else 1 - planar


def read_kernel(first, kinds, sens_mine, sens_theirs, *refs):
    count = len(kinds)
    blocks, hids, refs = refs[:count], refs[count : 2 * count], refs[2 * count :]
    owners = [owner_of(kind) for kind in kinds]
    before, refs = (None, refs) if first else (refs[0], refs[1:])
    total_ref, padded = refs
    rows = blocks[0].shape[0]
    spare = padded.shape[1] - rows
    tokens = sens_mine.shape[0]
    chunk = 256
    for i in range(count):
        padded[i, :spare] = jnp.zeros((spare, padded.shape[2]), padded.dtype)
        padded[i, rows:] = jnp.zeros((spare, padded.shape[2]), padded.dtype)
        padded[i, pl.ds(pl.multiple_of(owners[i] * spare, spare), rows)] = blocks[i][...]
        for at in range(0, 2 * tokens, chunk):
            sens = sens_mine if at < tokens else sens_theirs
            part = jnp.dot(hids[i][at : at + chunk], padded[i], preferred_element_type=jnp.float32)
            part = part * sens[at % tokens : at % tokens + chunk].astype(jnp.float32)
            lanes = [part[:, lane : lane + 128] for lane in range(0, part.shape[1], 128)]
            if i > 0:
                lanes.append(total_ref[at : at + chunk])
            elif not first:
                lanes.append(before[at : at + chunk])
            total_ref[at : at + chunk] = sum(lanes[1:], lanes[0])


def read_blocks(kinds, sens, blocks, hids, before, flops=0):
    vmem = pl.BlockSpec(memory_space=pltpu.VMEM)
    count = len(blocks)
    tokens, window = hids[0].shape
    earlier = [] if before is None else [before]
    return pl.pallas_call(
        functools.partial(read_kernel, before is None, kinds),
        in_specs=[vmem] * (2 + 2 * count + len(earlier)),
        out_specs=vmem,
        out_shape=jax.ShapeDtypeStruct((tokens, 128), jnp.float32),
        scratch_shapes=[pltpu.VMEM((count, window, blocks[0].shape[1]), hids[0].dtype)],
        cost_estimate=pl.CostEstimate(flops=flops, bytes_accessed=0, transcendentals=0),
        compiler_params=pltpu.CompilerParams(vmem_limit_bytes=VMEM_GRANT),
    )(*sens, *blocks, *hids, *earlier)


def shards(hidden_states, kv_weight, sensitivity, logp_shift, token_mask, lengths, rewards):
    seq_slots = hidden_states.shape[2]
    width = hidden_states.shape[3]
    columns = kv_weight.shape[1]
    rows = kv_weight.shape[0]
    scale_read = 0.3 / math.sqrt(columns)
    at = lax.axis_index("fsdp")
    core = at % NC
    y = (at // NC) % NY
    x = at // (NC * NY)
    first = core == 0
    f32, bf16 = jnp.float32, jnp.bfloat16

    hid_mine = hidden_states.reshape(-1, width)
    hid_theirs = to_core(hid_mine)
    tokens = hid_mine.shape[0]
    sens_mine = sensitivity.reshape(-1, columns)
    sens_theirs = to_core(sens_mine)

    next_y = jnp.where(first, 1, NY - 1)
    spots = {
        "own": (0, 0, "core"),
        "side": (1, 0, "core"),
        "near": (0, next_y, "plane"),
        "near_other": (0, next_y, "passed"),
        "near_side": (1, next_y, "plane"),
        "near_side_other": (1, next_y, "passed"),
        "far": (0, 2, "plane"),
        "far_side": (1, 2, "plane"),
    }
    window = -(-rows // 128) * 128
    spare = window - rows
    h, w = {}, {"own": kv_weight}

    def windows(*names):
        cut = []
        for name in names:
            dx, dy, owner = spots[name]
            start = ((x ^ dx) * NY + (y + dy) % NY) * NC * rows + owner_of(owner) * (rows - spare)
            both = [lax.dynamic_slice_in_dim(a, start, window, axis=1) for a in (hid_mine, hid_theirs)]
            cut.append(jnp.concatenate(both, axis=0))
        h.update(zip(names, lax.optimization_barrier(tuple(cut))))

    def read_terms(before, *names):
        return read_blocks(
            [spots[name][2] for name in names], (sens_mine, sens_theirs), [w[name] for name in names], [h[name] for name in names], before
        )

    w["near"] = rows_along_y(kv_weight, -1)
    w["side"] = along_x(kv_weight, -1)
    reward_vals = rewards.astype(f32)
    both = jnp.concatenate([reward_vals, reward_vals * reward_vals])
    sums = jnp.broadcast_to(jnp.sum(both, axis=1)[:, None, None], (2, reward_vals.shape[1], seq_slots))
    for bit in (1, 2):
        sums = sums + to_z_xor(sums, bit)

    near, w["side"], sums = lax.optimization_barrier((w["near"], w["side"], sums))
    w["near"] = near
    w["near_other"] = along_z(near)
    w["near_side"] = along_x(near, -1)
    w["far"] = along_y(near, -1)
    windows("own", "side")
    sums, h["own"] = lax.optimization_barrier((sums, h["own"]))
    sums = sums + to_z_xor(sums, 4)
    read = read_terms(None, "own", "side")

    near_side, far, _, read = lax.optimization_barrier((w["near_side"], w["far"], w["near_other"], read))
    w["near_side_other"] = along_z(near_side)
    w["far_side"] = along_x(far, -1)
    sums, read = lax.optimization_barrier((sums, read))
    reward_mean = sums[0] / GROUP_SIZE
    spread = jnp.sqrt(jnp.maximum(sums[1] / GROUP_SIZE - reward_mean * reward_mean, 0.0))
    advantage = (reward_vals[:, :, None] - reward_mean) / jnp.maximum(spread, 1.0)
    positions = lax.broadcasted_iota(jnp.int32, (1, 1, seq_slots), 2)
    kept = ((positions < lengths[:, :, None]) & (token_mask == 1)).astype(f32)
    coef = -LOSS_SCALE * advantage * kept / lengths[:, :, None].astype(f32)
    per_token = jnp.stack([logp_shift.reshape(-1), coef.reshape(-1)])
    windows("near", "near_other", "near_side", "far")
    read = read_terms(read, "near", "near_other", "near_side", "far")
    windows("near_side_other", "far_side")
    read = read_terms(read, "near_side_other", "far_side")
    read, per_token = lax.optimization_barrier((jnp.sum(read, axis=1), per_token))
    shift, coef = jnp.concatenate([per_token, to_core(per_token)], axis=1)

    read_theirs = to_core(read)
    read = read + jnp.concatenate([read_theirs[tokens:], read_theirs[:tokens]])
    ratios = jnp.exp(shift + scale_read * read)
    factor = jnp.clip(ratios, CLIP_LOW, CLIP_HIGH) * coef * scale_read
    sens = jnp.concatenate([sens_mine, sens_theirs], axis=0)
    step_dir = (factor[:, None] * sens.astype(f32)).astype(bf16)

    def term(name, step):
        out = lax.dot_general(h[name], step, (((0,), (0,)), ((), ())), preferred_element_type=f32)
        return name, lax.optimization_barrier(out)

    def add(named, *received):
        name, total = named
        spare = total.shape[0] - rows
        total = jnp.where(owner_of(spots[name][2]) == 0, total[:rows], total[spare:])
        for r in received:
            total = total + r.astype(f32)
        return total

    far_side = along_x(add(term("far_side", step_dir)).astype(bf16), 1)
    near_side_other = along_z(add(term("near_side_other", step_dir)).astype(bf16))
    far = term("far", step_dir)
    near_side = term("near_side", step_dir)
    near_other = add(term("near_other", step_dir)).astype(bf16)

    step, near_other = lax.optimization_barrier((step_dir, near_other, far_side, near_side_other))[:2]
    far = along_y(add(far, far_side).astype(bf16), 1)
    near_side = along_x(add(near_side, near_side_other).astype(bf16), 1)
    near_other = along_z(near_other)
    near = term("near", step)
    side = add(term("side", step)).astype(bf16)

    step, side = lax.optimization_barrier((step_dir, side, far, near_side, near_other))[:2]
    near = rows_along_y(add(near, near_side, far, near_other).astype(bf16), 1)
    side = along_x(side, 1)
    row_block = add(term("own", step), side, near)

    own = columns // NZ
    blocks = row_block.astype(bf16).reshape(rows, NZ, own).transpose(1, 0, 2)
    blocks = lax.all_to_all(blocks, "group", 0, 0)
    z = lax.axis_index("group")
    others = lax.broadcasted_iota(jnp.int32, (NZ, 1, 1), 0) != z
    total = jnp.sum(jnp.where(others, blocks.astype(f32), 0.0), axis=0)
    total = total + lax.dynamic_slice_in_dim(row_block, z * own, own, axis=1)
    return total + to_dp(total)


def solution(mesh):
    in_specs = (
        P(("fsdp", "dp"), "group", None, None),
        P("fsdp", None),
        P(("fsdp", "dp"), "group", None, None),
        P(("fsdp", "dp"), "group", None),
        P(("fsdp", "dp"), "group", None),
        P(("fsdp", "dp"), "group"),
        P(("fsdp", "dp"), "group"),
    )
    out_specs = P("fsdp", "group")
    return jax.shard_map(shards, mesh=mesh, in_specs=in_specs, out_specs=out_specs, check_vma=False)
```

profile of v0, /device:TPU:2, one launch (start us, length us, event | category | flops | bytes accessed | tf_op | source)
XLA Modules:
  0.0 127.6 jit_solution(16935815203291133378)
XLA Ops:
  0.0 3.0 %collective-permute-start = (bf16[320,1024]{1,0:T(8,128)(2,1)}, bf16[320,1024]{1,0:T(8,128)(2,1)S(1)}, u32[]{:S(2)}, u32[]{:S(2)}) collective-permute-start(bf16[320,1024]{1,0:T(8,128)(2,1)} %refs_0_.1), channel_id=1, source_target_pairs={{32,0},{50,2},{36,4},{54,6},{40,8},{58,10},{44,12},{62,14},{112,16... | collective-permute-start | bytes 1966088 | tf_op jit(solution)/shard_map/ppermute | solution.py:50
  5.7 1.8 %collective-permute-start.5 = (bf16[512,1024]{1,0:T(8,128)(2,1)}, bf16[512,1024]{1,0:T(8,128)(2,1)S(1)}, u32[]{:S(2)}, u32[]{:S(2)}) collective-permute-start(bf16[512,1024]{1,0:T(8,128)(2,1)} %bitcast.37), channel_id=1, source_target_pairs={{0,16},{16,0},{32,48},{48,32},{64,80},{80,64},{96,112},{112,96},{1... | collective-permute-start | bytes 3145736 | tf_op jit(solution)/shard_map/ppermute | solution.py:34
  7.5 1.2 collective-permute-done.2
  8.8 3.3 %collective-permute-start.3 = (f32[2,2,256]{2,1,0:T(2,128)S(1)}, f32[2,2,256]{2,1,0:T(2,128)S(1)}, u32[]{:S(2)}, u32[]{:S(2)}) collective-permute-start(f32[2,2,256]{2,1,0:T(2,128)S(1)} %broadcast_add_fusion), channel_id=1, source_target_pairs={{0,4},{2,6},{4,0},{6,2},{8,12},{10,14},{12,8},{14,10},{1,5},{3,7},... | collective-permute-start | bytes 12296 | tf_op jit(solution)/shard_map/ppermute | solution.py:72
  12.1 1.6 %collective-permute-done.3 = f32[2,2,256]{2,1,0:T(2,128)S(1)} collective-permute-done((f32[2,2,256]{2,1,0:T(2,128)S(1)}, f32[2,2,256]{2,1,0:T(2,128)S(1)}, u32[]{:S(2)}, u32[]{:S(2)}) %collective-permute-start.3) | collective-permute-done | bytes 4128 | tf_op jit(solution)/shard_map/ppermute | solution.py:72
  14.7 2.7 %collective-permute-start.6 = (bf16[320,1024]{1,0:T(8,128)(2,1)S(1)}, bf16[320,1024]{1,0:T(8,128)(2,1)}, u32[]{:S(2)}, u32[]{:S(2)}) collective-permute-start(bf16[320,1024]{1,0:T(8,128)(2,1)S(1)} %collective-permute-done.refs_0_), channel_id=1, source_target_pairs={{0,129},{1,128},{16,144},{17,145},{32,161},{33,160},{48,176},{49,1... | collective-permute-start | bytes 1966088 | tf_op jit(solution)/shard_map/ppermute | solution.py:68
  18.1 1.5 %collective-permute-start.8 = (bf16[320,1024]{1,0:T(8,128)(2,1)S(1)}, bf16[320,1024]{1,0:T(8,128)(2,1)S(1)}, u32[]{:S(2)}, u32[]{:S(2)}) collective-permute-start(bf16[320,1024]{1,0:T(8,128)(2,1)S(1)} %collective-permute-done.refs_0_), channel_id=1, source_target_pairs={{0,2},{2,0},{4,6},{6,4},{8,10},{10,8},{12,14},{14,12},{16,30},{18,... | collective-permute-start | bytes 1966088 | tf_op jit(solution)/shard_map/ppermute | solution.py:59
  19.6 3.7 %constant_dynamic-slice_fusion.9 = (bf16[512,384]{1,0:T(8,128)(2,1)}, bf16[512,384]{1,0:T(8,128)(2,1)}, bf16[512,384]{1,0:T(8,128)(2,1)}, bf16[512,384]{1,0:T(8,...) fusion(bf16[512,5120]{1,0:T(8,128)(2,1)} %bitcast.43, ...), kind=kLoop, calls=%fused_computation.46 | loop fusion | bytes 6291488 | tf_op jit(solution)/shard_map/dynamic_slice | solution.py:176
  23.3 2.3 %constant_dynamic-slice_fusion.8 = (bf16[512,384]{1,0:T(8,128)(2,1)S(1)}, bf16[512,384]{1,0:T(8,128)(2,1)S(1)}, bf16[512,384]{1,0:T(8,128)(2,1)S(1)}, bf16[512,3...) fusion(bf16[512,5120]{1,0:T(8,128)(2,1)} %collective-permute-do, ...), kind=kLoop, calls=%fused_computation.45 | loop fusion | bytes 6291488 | tf_op jit(solution)/shard_map/dynamic_slice | solution.py:176
  25.8 6.0 %collective-permute-start.11 = (f32[2,2,256]{2,1,0:T(2,128)S(1)}, f32[2,2,256]{2,1,0:T(2,128)S(1)}, u32[]{:S(2)}, u32[]{:S(2)}) collective-permute-start(f32[2,2,256]{2,1,0:T(2,128)S(1)} %fusion.49), channel_id=1, source_target_pairs={{0,8},{2,10},{4,12},{6,14},{8,0},{10,2},{12,4},{14,6},{1,9},{3,11}... | collective-permute-start | bytes 12296 | tf_op jit(solution)/shard_map/ppermute | solution.py:72
  31.9 2.5 %shard_map.76.refs_8_ = f32[1024,128]{1,0:T(8,128)S(1)} custom-call(bf16[512,1024]{1,0:T(8,128)(2,1)S(1)} %bitcast.38, bf16[512,1024]{1,0:T(8,128)(2,1)S(1)} %collective-permute-done.5.sens_theirs, bf16[320,1024]{1,0:T(8,128)(2,1)S(1)} %copy-done.17, bf16[320,1024]{1,0:T(8,128)(2,1)S(1)} %copy-done.19, bf16[1024,384]{1,0:T(8,128)(2,1)S(1)} %get-tuple-element.31.refs_2_, ...), custom_call_target="tpu_custom_call" | custom-call | tf_op jit(solution)/shard_map/pallas_call | solution.py:126
  34.4 2.3 %collective-permute-start.10 = (bf16[320,1024]{1,0:T(8,128)(2,1)}, bf16[320,1024]{1,0:T(8,128)(2,1)S(1)}, u32[]{:S(2)}, u32[]{:S(2)}) collective-permute-start(bf16[320,1024]{1,0:T(8,128)(2,1)} %collective-permute-done.7.refs_3_), channel_id=1, source_target_pairs={{0,129},{1,128},{16,144},{17,145},{32,161},{33,160},{48,176},{49,1... | collective-permute-start | bytes 1966088 | tf_op jit(solution)/shard_map/ppermute | solution.py:68
  36.7 1.4 %collective-permute-start.9 = (bf16[320,1024]{1,0:T(8,128)(2,1)}, bf16[320,1024]{1,0:T(8,128)(2,1)S(1)}, u32[]{:S(2)}, u32[]{:S(2)}) collective-permute-start(bf16[320,1024]{1,0:T(8,128)(2,1)} %collective-permute-done.6.refs_2_), channel_id=1, source_target_pairs={{0,2},{2,0},{4,6},{6,4},{8,10},{10,8},{12,14},{14,12},{16,30},{18,... | collective-permute-start | bytes 1966088 | tf_op jit(solution)/shard_map/ppermute | solution.py:59
  41.8 6.1 %shard_map.77.refs_4_ = f32[1024,128]{1,0:T(8,128)S(1)} custom-call(bf16[512,1024]{1,0:T(8,128)(2,1)S(1)} %bitcast.39, bf16[512,1024]{1,0:T(8,128)(2,1)S(1)} %collective-permute-done.5.sens_theirs, bf16[320,1024]{1,0:T(8,128)(2,1)S(1)} %collective-permute-done.refs_0_, bf16[320,1024]{1,0:T(8,128)(2,1)S(1)} %copy-done.16, ...), custom_call_target="tpu_custom_call" | custom-call | tf_op jit(solution)/shard_map/pallas_call | solution.py:126
  47.9 2.5 %shard_map.78 = f32[1024,128]{1,0:T(8,128)S(1)} custom-call(bf16[512,1024]{1,0:T(8,128)(2,1)S(1)} %bitcast.40, bf16[512,1024]{1,0:T(8,128)(2,1)S(1)} %collective-permute-done.5.sens_theirs, bf16[320,1024]{1,0:T(8,128)(2,1)S(1)} %collective-permute-done.9.refs_0_, bf16[320,1024]{1,0:T(8,128)(2,1)S(1)} %collective-permute-done.10.refs_1_, ...), custom_call_target="tpu_custom_call" | custom-call | tf_op jit(solution)/shard_map/pallas_call | solution.py:126
  54.3 1.0 fusion.26
  56.5 1.1 collective-permute-start.15
  58.0 1.0 fusion.25
  59.1 1.0 fusion.29
  60.1 7.1 %collective-permute-done.15 = bf16[320,1024]{1,0:T(8,128)(2,1)S(1)} collective-permute-done((bf16[320,1024]{1,0:T(8,128)(2,1)S(1)}, bf16[320,1024]{1,0:T(8,128)(2,1)S(1)}, u32[]{:S(2)}, u32[]{:S(2)}) %collective-permute-start.15) | collective-permute-done | bytes 655392 | tf_op jit(solution)/shard_map/ppermute | solution.py:59
  67.2 1.4 %collective-permute-done.14 = bf16[320,1024]{1,0:T(8,128)(2,1)S(1)} collective-permute-done((bf16[320,1024]{1,0:T(8,128)(2,1)S(1)}, bf16[320,1024]{1,0:T(8,128)(2,1)S(1)}, u32[]{:S(2)}, u32[]{:S(2)}) %collective-permute-start.14) | collective-permute-done | bytes 655392 | tf_op jit(solution)/shard_map/ppermute | solution.py:68
  69.2 1.4 %collective-permute-start.16 = (bf16[320,1024]{1,0:T(8,128)(2,1)S(1)}, bf16[320,1024]{1,0:T(8,128)(2,1)S(1)}, u32[]{:S(2)}, u32[]{:S(2)}) collective-permute-start(bf16[320,1024]{1,0:T(8,128)(2,1)S(1)} %fusion.9), channel_id=1, source_target_pairs={{0,32},{16,112},{32,64},{48,16},{64,96},{80,48},{96,0},{112,80},{1... | collective-permute-start | bytes 1966088 | tf_op jit(solution)/shard_map/ppermute | solution.py:39
  72.6 1.0 fusion.32
  73.7 5.8 %collective-permute-done.17 = bf16[320,1024]{1,0:T(8,128)(2,1)S(1)} collective-permute-done((bf16[320,1024]{1,0:T(8,128)(2,1)S(1)}, bf16[320,1024]{1,0:T(8,128)(2,1)S(1)}, u32[]{:S(2)}, u32[]{:S(2)}) %collective-permute-start.17) | collective-permute-done | bytes 655392 | tf_op jit(solution)/shard_map/ppermute | solution.py:68
  79.5 1.6 %collective-permute-done.16 = bf16[320,1024]{1,0:T(8,128)(2,1)S(1)} collective-permute-done((bf16[320,1024]{1,0:T(8,128)(2,1)S(1)}, bf16[320,1024]{1,0:T(8,128)(2,1)S(1)}, u32[]{:S(2)}, u32[]{:S(2)}) %collective-permute-start.16) | collective-permute-done | bytes 655392 | tf_op jit(solution)/shard_map/ppermute | solution.py:39
  82.4 1.0 fusion.31
  83.5 8.3 %collective-permute-done.19 = bf16[320,1024]{1,0:T(8,128)(2,1)S(1)} collective-permute-done((bf16[320,1024]{1,0:T(8,128)(2,1)S(1)}, bf16[320,1024]{1,0:T(8,128)(2,1)S(1)}, u32[]{:S(2)}, u32[]{:S(2)}) %collective-permute-start.19) | collective-permute-done | bytes 655392 | tf_op jit(solution)/shard_map/ppermute | solution.py:68
  91.7 2.4 %collective-permute-done.20 = bf16[320,1024]{1,0:T(8,128)(2,1)S(1)} collective-permute-done((bf16[320,1024]{1,0:T(8,128)(2,1)S(1)}, bf16[320,1024]{1,0:T(8,128)(2,1)S(1)}, u32[]{:S(2)}, u32[]{:S(2)}) %collective-permute-start.20) | collective-permute-done | bytes 655392 | tf_op jit(solution)/shard_map/ppermute | solution.py:50
  95.5 3.5 %all-to-all-start = ((bf16[8,320,128]{2,1,0:T(8,128)(2,1)}), bf16[8,320,128]{2,1,0:T(8,128)(2,1)S(1)}, u32[]{:S(2)}, u32[]{:S(2)}) async-start(bf16[8,320,128]{2,1,0:T(8,128)(2,1)} %bitcast.36), calls=%async_computation | async-start | bytes 1310720 | tf_op jit(solution)/shard_map/all_to_all | solution.py:260
  99.1 19.9 %all-to-all-done = bf16[8,320,128]{2,1,0:T(8,128)(2,1)S(1)} async-done(((bf16[8,320,128]{2,1,0:T(8,128)(2,1)}), bf16[8,320,128]{2,1,0:T(8,128)(2,1)S(1)}, u32[]{:S(2)}, u32[]{:S(2)}) %all-to-all-start) | async-done | bytes 655392 | tf_op jit(solution)/shard_map/all_to_all | solution.py:260
  119.2 2.3 %collective-permute-start.21 = (f32[320,128]{1,0:T(8,128)S(1)}, f32[320,128]{1,0:T(8,128)S(1)}, u32[]{:S(2)}, u32[]{:S(2)}) collective-permute-start(f32[320,128]{1,0:T(8,128)S(1)} %dynamic-slice_add_fusion), channel_id=1, source_target_pairs={{0,1},{1,0},{2,3},{3,2},{4,5},{5,4},{6,7},{7,6},{8,9},{9,8},{10,11... | collective-permute-start | bytes 491528 | tf_op jit(solution)/shard_map/ppermute | solution.py:76
  121.5 5.4 %collective-permute-done.21 = f32[320,128]{1,0:T(8,128)S(1)} collective-permute-done((f32[320,128]{1,0:T(8,128)S(1)}, f32[320,128]{1,0:T(8,128)S(1)}, u32[]{:S(2)}, u32[]{:S(2)}) %collective-permute-start.21) | collective-permute-done | bytes 163872 | tf_op jit(solution)/shard_map/ppermute | solution.py:76
  (125 shorter events, 20.0 us)
Async XLA Ops:
  0.0 23.3 %collective-permute-start.4 = (bf16[512,5120]{1,0:T(8,128)(2,1)}, bf16[512,5120]{1,0:T(8,128)(2,1)}, u32[]{:S(2)}, u32[]{:S(2)}) collective-permute-start(bf16[512,5120]{1,0:T(8,128)(2,1)} %bitcast.42), channel_id=1, source_target_pairs={{0,16},{16,0},{32,48},{48,32},{64,80},{80,64},{96,112},{112,96},{1... | collective-permute-start | bytes 15728648 | tf_op jit(solution)/shard_map/ppermute | solution.py:34
  0.0 13.8 %collective-permute-start = (bf16[320,1024]{1,0:T(8,128)(2,1)}, bf16[320,1024]{1,0:T(8,128)(2,1)S(1)}, u32[]{:S(2)}, u32[]{:S(2)}) collective-permute-start(bf16[320,1024]{1,0:T(8,128)(2,1)} %refs_0_.1), channel_id=1, source_target_pairs={{32,0},{50,2},{36,4},{54,6},{40,8},{58,10},{44,12},{62,14},{112,16... | collective-permute-start | bytes 1966088 | tf_op jit(solution)/shard_map/ppermute | solution.py:50
  3.0 10.8 %collective-permute-start.1 = (bf16[320,1024]{1,0:T(8,128)(2,1)}, bf16[320,1024]{1,0:T(8,128)(2,1)S(1)}, u32[]{:S(2)}, u32[]{:S(2)}) collective-permute-start(bf16[320,1024]{1,0:T(8,128)(2,1)} %refs_0_.1), channel_id=1, source_target_pairs={{0,129},{1,128},{16,144},{17,145},{32,161},{33,160},{48,176},{49,1... | collective-permute-start | bytes 1966088 | tf_op jit(solution)/shard_map/ppermute | solution.py:68
  5.1 3.7 %collective-permute-start.2 = (f32[2,2,256]{2,1,0:T(2,128)S(1)}, f32[2,2,256]{2,1,0:T(2,128)S(1)}, u32[]{:S(2)}, u32[]{:S(2)}) collective-permute-start(f32[2,2,256]{2,1,0:T(2,128)S(1)} %broadcast_in_dim.11), channel_id=1, source_target_pairs={{0,2},{2,0},{4,6},{6,4},{8,10},{10,8},{12,14},{14,12},{1,3},{3,1},... | collective-permute-start | bytes 12296 | tf_op jit(solution)/shard_map/ppermute | solution.py:72
  5.7 26.2 %collective-permute-start.5 = (bf16[512,1024]{1,0:T(8,128)(2,1)}, bf16[512,1024]{1,0:T(8,128)(2,1)S(1)}, u32[]{:S(2)}, u32[]{:S(2)}) collective-permute-start(bf16[512,1024]{1,0:T(8,128)(2,1)} %bitcast.37), channel_id=1, source_target_pairs={{0,16},{16,0},{32,48},{48,32},{64,80},{80,64},{96,112},{112,96},{1... | collective-permute-start | bytes 3145736 | tf_op jit(solution)/shard_map/ppermute | solution.py:34
  8.8 4.9 %collective-permute-start.3 = (f32[2,2,256]{2,1,0:T(2,128)S(1)}, f32[2,2,256]{2,1,0:T(2,128)S(1)}, u32[]{:S(2)}, u32[]{:S(2)}) collective-permute-start(f32[2,2,256]{2,1,0:T(2,128)S(1)} %broadcast_add_fusion), channel_id=1, source_target_pairs={{0,4},{2,6},{4,0},{6,2},{8,12},{10,14},{12,8},{14,10},{1,5},{3,7},... | collective-permute-start | bytes 12296 | tf_op jit(solution)/shard_map/ppermute | solution.py:72
  13.8 9.5 %copy-start.29 = (f32[1,2,256]{2,1,0:T(2,128)S(1)}, f32[1,2,256]{2,1,0:T(2,128)}, u32[]{:S(2)}) copy-start(f32[1,2,256]{2,1,0:T(2,128)} %param.10) | copy-start | bytes 6148
  13.8 9.5 %copy-start.30 = (s32[1,2]{1,0:T(1,128)S(1)}, s32[1,2]{1,0:T(1,128)}, u32[]{:S(2)}) copy-start(s32[1,2]{1,0:T(1,128)} %param.12) | copy-start | bytes 28
  14.7 19.7 %collective-permute-start.6 = (bf16[320,1024]{1,0:T(8,128)(2,1)S(1)}, bf16[320,1024]{1,0:T(8,128)(2,1)}, u32[]{:S(2)}, u32[]{:S(2)}) collective-permute-start(bf16[320,1024]{1,0:T(8,128)(2,1)S(1)} %collective-permute-done.refs_0_), channel_id=1, source_target_pairs={{0,129},{1,128},{16,144},{17,145},{32,161},{33,160},{48,176},{49,1... | collective-permute-start | bytes 1966088 | tf_op jit(solution)/shard_map/ppermute | solution.py:68
  17.3 17.1 %collective-permute-start.7 = (bf16[320,1024]{1,0:T(8,128)(2,1)S(1)}, bf16[320,1024]{1,0:T(8,128)(2,1)}, u32[]{:S(2)}, u32[]{:S(2)}) collective-permute-start(bf16[320,1024]{1,0:T(8,128)(2,1)S(1)} %collective-permute-done.refs_0_), channel_id=1, source_target_pairs={{0,96},{16,48},{32,0},{48,80},{64,32},{80,112},{96,64},{112,16},{1... | collective-permute-start | bytes 1966088 | tf_op jit(solution)/shard_map/ppermute | solution.py:39
  18.1 16.3 %collective-permute-start.8 = (bf16[320,1024]{1,0:T(8,128)(2,1)S(1)}, bf16[320,1024]{1,0:T(8,128)(2,1)S(1)}, u32[]{:S(2)}, u32[]{:S(2)}) collective-permute-start(bf16[320,1024]{1,0:T(8,128)(2,1)S(1)} %collective-permute-done.refs_0_), channel_id=1, source_target_pairs={{0,2},{2,0},{4,6},{6,4},{8,10},{10,8},{12,14},{14,12},{16,30},{18,... | collective-permute-start | bytes 1966088 | tf_op jit(solution)/shard_map/ppermute | solution.py:59
  25.6 6.3 %copy-start = (bf16[1,2,256,1024]{3,2,1,0:T(8,128)(2,1)S(1)}, bf16[1,2,256,1024]{3,2,1,0:T(8,128)(2,1)}, u32[]{:S(2)}) copy-start(bf16[1,2,256,1024]{3,2,1,0:T(8,128)(2,1)} %param.9) | copy-start | bytes 3145732
  25.8 8.6 %copy-start.1 = (bf16[1024,384]{1,0:T(8,128)(2,1)}, bf16[1024,384]{1,0:T(8,128)(2,1)S(1)}, u32[]{:S(2)}) copy-start(bf16[1024,384]{1,0:T(8,128)(2,1)S(1)} %get-tuple-element.34.refs_3_) | copy-start | bytes 2359300
  25.8 8.6 %copy-start.13 = (bf16[1024,384]{1,0:T(8,128)(2,1)}, bf16[1024,384]{1,0:T(8,128)(2,1)S(1)}, u32[]{:S(2)}) copy-start(bf16[1024,384]{1,0:T(8,128)(2,1)S(1)} %get-tuple-element.31.refs_2_) | copy-start | bytes 2359300
  25.8 15.0 %collective-permute-start.11 = (f32[2,2,256]{2,1,0:T(2,128)S(1)}, f32[2,2,256]{2,1,0:T(2,128)S(1)}, u32[]{:S(2)}, u32[]{:S(2)}) collective-permute-start(f32[2,2,256]{2,1,0:T(2,128)S(1)} %fusion.49), channel_id=1, source_target_pairs={{0,8},{2,10},{4,12},{6,14},{8,0},{10,2},{12,4},{14,6},{1,9},{3,11}... | collective-permute-start | bytes 12296 | tf_op jit(solution)/shard_map/ppermute | solution.py:72
  31.9 6.3 %copy-start.24 = (bf16[512,384]{1,0:T(8,128)(2,1)S(1)}, bf16[512,384]{1,0:T(8,128)(2,1)}, u32[]{:S(2)}) copy-start(bf16[512,384]{1,0:T(8,128)(2,1)} %get-tuple-element.56) | copy-start | bytes 1179652
  34.4 13.4 %collective-permute-start.10 = (bf16[320,1024]{1,0:T(8,128)(2,1)}, bf16[320,1024]{1,0:T(8,128)(2,1)S(1)}, u32[]{:S(2)}, u32[]{:S(2)}) collective-permute-start(bf16[320,1024]{1,0:T(8,128)(2,1)} %collective-permute-done.7.refs_3_), channel_id=1, source_target_pairs={{0,129},{1,128},{16,144},{17,145},{32,161},{33,160},{48,176},{49,1... | collective-permute-start | bytes 1966088 | tf_op jit(solution)/shard_map/ppermute | solution.py:68
  36.7 11.1 %collective-permute-start.9 = (bf16[320,1024]{1,0:T(8,128)(2,1)}, bf16[320,1024]{1,0:T(8,128)(2,1)S(1)}, u32[]{:S(2)}, u32[]{:S(2)}) collective-permute-start(bf16[320,1024]{1,0:T(8,128)(2,1)} %collective-permute-done.6.refs_2_), channel_id=1, source_target_pairs={{0,2},{2,0},{4,6},{6,4},{8,10},{10,8},{12,14},{14,12},{16,30},{18,... | collective-permute-start | bytes 1966088 | tf_op jit(solution)/shard_map/ppermute | solution.py:59
  40.8 7.1 %copy-start.9 = (bf16[1024,384]{1,0:T(8,128)(2,1)}, bf16[1024,384]{1,0:T(8,128)(2,1)S(1)}, u32[]{:S(2)}) copy-start(bf16[1024,384]{1,0:T(8,128)(2,1)S(1)} %get-tuple-element.38.refs_3_) | copy-start | bytes 2359300
  40.8 7.1 %copy-start.11 = (bf16[1024,384]{1,0:T(8,128)(2,1)}, bf16[1024,384]{1,0:T(8,128)(2,1)S(1)}, u32[]{:S(2)}) copy-start(bf16[1024,384]{1,0:T(8,128)(2,1)S(1)} %get-tuple-element.37.refs_2_) | copy-start | bytes 2359300
  50.6 1.3 collective-permute-start.12
  50.7 1.3 %collective-permute-start.13 = (f32[1024]{0:T(1024)S(1)}, f32[1024]{0:T(1024)S(1)}, u32[]{:S(2)}, u32[]{:S(2)}) collective-permute-start(f32[1024]{0:T(1024)S(1)} %reduce_sum.28), channel_id=1, source_target_pairs={{0,16},{16,0},{32,48},{48,32},{64,80},{80,64},{96,112},{112,96},{1... | collective-permute-start | bytes 12296 | tf_op jit(solution)/shard_map/ppermute | solution.py:34
  56.5 10.7 %collective-permute-start.15 = (bf16[320,1024]{1,0:T(8,128)(2,1)S(1)}, bf16[320,1024]{1,0:T(8,128)(2,1)S(1)}, u32[]{:S(2)}, u32[]{:S(2)}) collective-permute-start(bf16[320,1024]{1,0:T(8,128)(2,1)S(1)} %fusion.11), channel_id=1, source_target_pairs={{0,2},{2,0},{4,6},{6,4},{8,10},{10,8},{12,14},{14,12},{16,30},{18,... | collective-permute-start | bytes 1966088 | tf_op jit(solution)/shard_map/ppermute | solution.py:59
  57.7 10.9 %collective-permute-start.14 = (bf16[320,1024]{1,0:T(8,128)(2,1)S(1)}, bf16[320,1024]{1,0:T(8,128)(2,1)S(1)}, u32[]{:S(2)}, u32[]{:S(2)}) collective-permute-start(bf16[320,1024]{1,0:T(8,128)(2,1)S(1)} %fusion.12), channel_id=1, source_target_pairs={{0,128},{1,129},{16,145},{17,144},{32,160},{33,161},{48,177},{49,1... | collective-permute-start | bytes 1966088 | tf_op jit(solution)/shard_map/ppermute | solution.py:68
  68.8 10.7 %collective-permute-start.17 = (bf16[320,1024]{1,0:T(8,128)(2,1)S(1)}, bf16[320,1024]{1,0:T(8,128)(2,1)S(1)}, u32[]{:S(2)}, u32[]{:S(2)}) collective-permute-start(bf16[320,1024]{1,0:T(8,128)(2,1)S(1)} %fusion.7), channel_id=1, source_target_pairs={{0,128},{1,129},{16,145},{17,144},{32,160},{33,161},{48,177},{49,1... | collective-permute-start | bytes 1966088 | tf_op jit(solution)/shard_map/ppermute | solution.py:68
  69.2 11.9 %collective-permute-start.16 = (bf16[320,1024]{1,0:T(8,128)(2,1)S(1)}, bf16[320,1024]{1,0:T(8,128)(2,1)S(1)}, u32[]{:S(2)}, u32[]{:S(2)}) collective-permute-start(bf16[320,1024]{1,0:T(8,128)(2,1)S(1)} %fusion.9), channel_id=1, source_target_pairs={{0,32},{16,112},{32,64},{48,16},{64,96},{80,48},{96,0},{112,80},{1... | collective-permute-start | bytes 1966088 | tf_op jit(solution)/shard_map/ppermute | solution.py:39
  70.6 10.6 %collective-permute-start.18 = (bf16[320,1024]{1,0:T(8,128)(2,1)S(1)}, bf16[320,1024]{1,0:T(8,128)(2,1)S(1)}, u32[]{:S(2)}, u32[]{:S(2)}) collective-permute-start(bf16[320,1024]{1,0:T(8,128)(2,1)S(1)} %fusion.13), channel_id=1, source_target_pairs={{0,2},{2,0},{4,6},{6,4},{8,10},{10,8},{12,14},{14,12},{16,30},{18,... | collective-permute-start | bytes 1966088 | tf_op jit(solution)/shard_map/ppermute | solution.py:59
  73.7 8.8 %copy-start.14 = (bf16[1024,384]{1,0:T(8,128)(2,1)S(1)}, bf16[1024,384]{1,0:T(8,128)(2,1)}, u32[]{:S(2)}) copy-start(bf16[1024,384]{1,0:T(8,128)(2,1)} %copy-done.13) | copy-start | bytes 2359300
  81.1 10.6 %collective-permute-start.19 = (bf16[320,1024]{1,0:T(8,128)(2,1)S(1)}, bf16[320,1024]{1,0:T(8,128)(2,1)S(1)}, u32[]{:S(2)}, u32[]{:S(2)}) collective-permute-start(bf16[320,1024]{1,0:T(8,128)(2,1)S(1)} %fusion.10), channel_id=1, source_target_pairs={{0,128},{1,129},{16,145},{17,144},{32,160},{33,161},{48,177},{49,1... | collective-permute-start | bytes 1966088 | tf_op jit(solution)/shard_map/ppermute | solution.py:68
  82.3 11.9 %collective-permute-start.20 = (bf16[320,1024]{1,0:T(8,128)(2,1)S(1)}, bf16[320,1024]{1,0:T(8,128)(2,1)S(1)}, u32[]{:S(2)}, u32[]{:S(2)}) collective-permute-start(bf16[320,1024]{1,0:T(8,128)(2,1)S(1)} %fusion.3), channel_id=1, source_target_pairs={{0,32},{2,50},{4,36},{6,54},{8,40},{10,58},{12,44},{14,62},{16,112... | collective-permute-start | bytes 1966088 | tf_op jit(solution)/shard_map/ppermute | solution.py:50
  95.5 23.5 %all-to-all-start = ((bf16[8,320,128]{2,1,0:T(8,128)(2,1)}), bf16[8,320,128]{2,1,0:T(8,128)(2,1)S(1)}, u32[]{:S(2)}, u32[]{:S(2)}) async-start(bf16[8,320,128]{2,1,0:T(8,128)(2,1)} %bitcast.36), calls=%async_computation | async-start | bytes 1310720 | tf_op jit(solution)/shard_map/all_to_all | solution.py:260
  119.2 7.7 %collective-permute-start.21 = (f32[320,128]{1,0:T(8,128)S(1)}, f32[320,128]{1,0:T(8,128)S(1)}, u32[]{:S(2)}, u32[]{:S(2)}) collective-permute-start(f32[320,128]{1,0:T(8,128)S(1)} %dynamic-slice_add_fusion), channel_id=1, source_target_pairs={{0,1},{1,0},{2,3},{3,2},{4,5},{5,4},{6,7},{7,6},{8,9},{9,8},{10,11... | collective-permute-start | bytes 491528 | tf_op jit(solution)/shard_map/ppermute | solution.py:76
  (22 other events, 53.2 us)
where the time goes:
time: 128 us
  waiting for transfers between devices  55.7 us (44%)
  starting transfers between devices  35 us (27%)
  local copies, waits for them, and re-layouts  11.9 us (9%)
  Pallas kernels  11 us (9%)
  matrix products  8.09 us (6%)
  other arithmetic  5.39 us (4%)
    all_to_all x1, waiting for transfers between devices, shards(): blocks = lax.all_to_all(blocks, 'group', 0, 0)  19.9 us
    ppermute x6, waiting for transfers between devices, along_x(): return lax.ppermute(a, ('fsdp', 'dp'), pairs)  15.5 us
    pallas_call x3, Pallas kernels, read_blocks(): pl.pallas_call(functools.partial(read_kernel, before is None, kinds), in_...  11 us
    ppermute x3, starting transfers between devices, to_z_xor(): return lax.ppermute(a, 'group', [(z, z ^ bit) for z in range(NZ)])  9.91 us
    dot_general x8, matrix products, term(): lax.dot_general(h[name], step, (((0,), (0,)), ((), ())), preferred_elemen...  8.09 us
    ppermute x4, waiting for transfers between devices, along_z(): return lax.ppermute(a, ('fsdp', 'group'), pairs)  7.16 us
    ppermute x6, starting transfers between devices, along_x(): return lax.ppermute(a, ('fsdp', 'dp'), pairs)  6.5 us
    dynamic_slice x2, local copies, waits for them, and re-layouts, windows(): lax.dynamic_slice_in_dim(a, start, window, axis=1)  5.94 us
  transfers between devices with their start and end apart: 23, of which 13 were waited for; matrix products, arithmetic and copies ran while one was open for 11% of the time, Pallas kernels for 7%

commit v1 on v0

--- a/solution.py
+++ b/solution.py
@@ -258,10 +258,7 @@
     own = columns // NZ
     blocks = row_block.astype(bf16).reshape(rows, NZ, own).transpose(1, 0, 2)
     blocks = lax.all_to_all(blocks, "group", 0, 0)
-    z = lax.axis_index("group")
-    others = lax.broadcasted_iota(jnp.int32, (NZ, 1, 1), 0) != z
-    total = jnp.sum(jnp.where(others, blocks.astype(f32), 0.0), axis=0)
-    total = total + lax.dynamic_slice_in_dim(row_block, z * own, own, axis=1)
+    total = jnp.sum(blocks.astype(f32), axis=0)
     return total + to_dp(total)
 
 

time: 128 us -> 127 us (level)
  blocking collectives: 0 us -> 23.3 us
  waiting for transfers between devices: 55.7 us -> 35 us
  starting transfers between devices: 35 us -> 31.4 us
    all_to_all x0 -> x1, blocking collectives: none -> 23.3 us  [shards(): blocks = lax.all_to_all(blocks, 'group', 0, 0)]
    all_to_all x1 -> x0, waiting for transfers between devices: 19.9 us -> none  [shards(): blocks = lax.all_to_all(blocks, 'group', 0, 0)]
    all_to_all x1 -> x0, starting transfers between devices: 3.54 us -> none  [shards(): blocks = lax.all_to_all(blocks, 'group', 0, 0)]
  transfers between devices with their start and end apart: 23 -> 22, of which waited for: 13 -> 12; matrix products, arithmetic and copies ran while one was open for 11% -> 11% of each run, Pallas kernels for 7% -> 7%
where the time goes in v1:
time: 127 us; the launch traced here: 125 us
  waiting for transfers between devices  35 us (28%)
  starting transfers between devices  31.4 us (25%)
  blocking collectives  23.3 us (18%)
  Pallas kernels  11 us (9%)
  local copies, waits for them, and re-layouts  10.9 us (9%)
  matrix products  8.09 us (6%)
  other arithmetic  5.14 us (4%)
    all_to_all x1, blocking collectives, shards(): blocks = lax.all_to_all(blocks, 'group', 0, 0)  23.3 us
    ppermute x6, waiting for transfers between devices, along_x(): return lax.ppermute(a, ('fsdp', 'dp'), pairs)  15.5 us
    pallas_call x3, Pallas kernels, read_blocks(): pl.pallas_call(functools.partial(read_kernel, before is None, kinds), in_...  11 us
    ppermute x3, starting transfers between devices, to_z_xor(): return lax.ppermute(a, 'group', [(z, z ^ bit) for z in range(NZ)])  9.91 us
    dot_general x8, matrix products, term(): lax.dot_general(h[name], step, (((0,), (0,)), ((), ())), preferred_elemen...  8.09 us
    ppermute x4, waiting for transfers between devices, along_z(): return lax.ppermute(a, ('fsdp', 'group'), pairs)  7.16 us
    ppermute x6, starting transfers between devices, along_x(): return lax.ppermute(a, ('fsdp', 'dp'), pairs)  6.49 us
    dynamic_slice x2, local copies, waits for them, and re-layouts, windows(): lax.dynamic_slice_in_dim(a, start, window, axis=1)  5.93 us
  transfers between devices with their start and end apart: 22, of which 12 were waited for; matrix products, arithmetic and copies ran while one was open for 11% of the time, Pallas kernels for 7%

profile of v1, /device:TPU:2, one launch (start us, length us, event | category | flops | bytes accessed | tf_op | source)
XLA Modules:
  0.0 125.4 jit_solution(13042263760508659010)
XLA Ops:
  0.0 3.0 %collective-permute-start = (bf16[320,1024]{1,0:T(8,128)(2,1)}, bf16[320,1024]{1,0:T(8,128)(2,1)S(1)}, u32[]{:S(2)}, u32[]{:S(2)}) collective-permute-start(bf16[320,1024]{1,0:T(8,128)(2,1)} %refs_0_.1), channel_id=1, source_target_pairs={{32,0},{50,2},{36,4},{54,6},{40,8},{58,10},{44,12},{62,14},{112,16... | collective-permute-start | bytes 1966088 | tf_op jit(solution)/shard_map/ppermute | solution.py:50
  5.7 1.8 %collective-permute-start.5 = (bf16[512,1024]{1,0:T(8,128)(2,1)}, bf16[512,1024]{1,0:T(8,128)(2,1)S(1)}, u32[]{:S(2)}, u32[]{:S(2)}) collective-permute-start(bf16[512,1024]{1,0:T(8,128)(2,1)} %bitcast.36), channel_id=1, source_target_pairs={{0,16},{16,0},{32,48},{48,32},{64,80},{80,64},{96,112},{112,96},{1... | collective-permute-start | bytes 3145736 | tf_op jit(solution)/shard_map/ppermute | solution.py:34
  7.5 1.2 collective-permute-done.2
  8.8 3.3 %collective-permute-start.3 = (f32[2,2,256]{2,1,0:T(2,128)S(1)}, f32[2,2,256]{2,1,0:T(2,128)S(1)}, u32[]{:S(2)}, u32[]{:S(2)}) collective-permute-start(f32[2,2,256]{2,1,0:T(2,128)S(1)} %broadcast_add_fusion), channel_id=1, source_target_pairs={{0,4},{2,6},{4,0},{6,2},{8,12},{10,14},{12,8},{14,10},{1,5},{3,7},... | collective-permute-start | bytes 12296 | tf_op jit(solution)/shard_map/ppermute | solution.py:72
  12.1 1.6 %collective-permute-done.3 = f32[2,2,256]{2,1,0:T(2,128)S(1)} collective-permute-done((f32[2,2,256]{2,1,0:T(2,128)S(1)}, f32[2,2,256]{2,1,0:T(2,128)S(1)}, u32[]{:S(2)}, u32[]{:S(2)}) %collective-permute-start.3) | collective-permute-done | bytes 4128 | tf_op jit(solution)/shard_map/ppermute | solution.py:72
  14.7 2.7 %collective-permute-start.6 = (bf16[320,1024]{1,0:T(8,128)(2,1)S(1)}, bf16[320,1024]{1,0:T(8,128)(2,1)}, u32[]{:S(2)}, u32[]{:S(2)}) collective-permute-start(bf16[320,1024]{1,0:T(8,128)(2,1)S(1)} %collective-permute-done.refs_0_), channel_id=1, source_target_pairs={{0,129},{1,128},{16,144},{17,145},{32,161},{33,160},{48,176},{49,1... | collective-permute-start | bytes 1966088 | tf_op jit(solution)/shard_map/ppermute | solution.py:68
  18.1 1.5 %collective-permute-start.8 = (bf16[320,1024]{1,0:T(8,128)(2,1)S(1)}, bf16[320,1024]{1,0:T(8,128)(2,1)S(1)}, u32[]{:S(2)}, u32[]{:S(2)}) collective-permute-start(bf16[320,1024]{1,0:T(8,128)(2,1)S(1)} %collective-permute-done.refs_0_), channel_id=1, source_target_pairs={{0,2},{2,0},{4,6},{6,4},{8,10},{10,8},{12,14},{14,12},{16,30},{18,... | collective-permute-start | bytes 1966088 | tf_op jit(solution)/shard_map/ppermute | solution.py:59
  19.6 3.7 %constant_dynamic-slice_fusion.9 = (bf16[512,384]{1,0:T(8,128)(2,1)}, bf16[512,384]{1,0:T(8,128)(2,1)}, bf16[512,384]{1,0:T(8,128)(2,1)}, bf16[512,384]{1,0:T(8,...) fusion(bf16[512,5120]{1,0:T(8,128)(2,1)} %bitcast.42, ...), kind=kLoop, calls=%fused_computation.54 | loop fusion | bytes 6291488 | tf_op jit(solution)/shard_map/dynamic_slice | solution.py:176
  23.3 2.3 %constant_dynamic-slice_fusion.8 = (bf16[512,384]{1,0:T(8,128)(2,1)S(1)}, bf16[512,384]{1,0:T(8,128)(2,1)S(1)}, bf16[512,384]{1,0:T(8,128)(2,1)S(1)}, bf16[512,3...) fusion(bf16[512,5120]{1,0:T(8,128)(2,1)} %collective-permute-do, ...), kind=kLoop, calls=%fused_computation.53 | loop fusion | bytes 6291488 | tf_op jit(solution)/shard_map/dynamic_slice | solution.py:176
  25.8 6.0 %collective-permute-start.11 = (f32[2,2,256]{2,1,0:T(2,128)S(1)}, f32[2,2,256]{2,1,0:T(2,128)S(1)}, u32[]{:S(2)}, u32[]{:S(2)}) collective-permute-start(f32[2,2,256]{2,1,0:T(2,128)S(1)} %fusion.50), channel_id=1, source_target_pairs={{0,8},{2,10},{4,12},{6,14},{8,0},{10,2},{12,4},{14,6},{1,9},{3,11}... | collective-permute-start | bytes 12296 | tf_op jit(solution)/shard_map/ppermute | solution.py:72
  31.9 2.5 %shard_map.76.refs_8_ = f32[1024,128]{1,0:T(8,128)S(1)} custom-call(bf16[512,1024]{1,0:T(8,128)(2,1)S(1)} %bitcast.37, bf16[512,1024]{1,0:T(8,128)(2,1)S(1)} %collective-permute-done.5.sens_theirs, bf16[320,1024]{1,0:T(8,128)(2,1)S(1)} %copy-done.17, bf16[320,1024]{1,0:T(8,128)(2,1)S(1)} %copy-done.19, bf16[1024,384]{1,0:T(8,128)(2,1)S(1)} %get-tuple-element.31.refs_2_, ...), custom_call_target="tpu_custom_call" | custom-call | tf_op jit(solution)/shard_map/pallas_call | solution.py:126
  34.4 2.3 %collective-permute-start.10 = (bf16[320,1024]{1,0:T(8,128)(2,1)}, bf16[320,1024]{1,0:T(8,128)(2,1)S(1)}, u32[]{:S(2)}, u32[]{:S(2)}) collective-permute-start(bf16[320,1024]{1,0:T(8,128)(2,1)} %collective-permute-done.7.refs_3_), channel_id=1, source_target_pairs={{0,129},{1,128},{16,144},{17,145},{32,161},{33,160},{48,176},{49,1... | collective-permute-start | bytes 1966088 | tf_op jit(solution)/shard_map/ppermute | solution.py:68
  36.7 1.4 %collective-permute-start.9 = (bf16[320,1024]{1,0:T(8,128)(2,1)}, bf16[320,1024]{1,0:T(8,128)(2,1)S(1)}, u32[]{:S(2)}, u32[]{:S(2)}) collective-permute-start(bf16[320,1024]{1,0:T(8,128)(2,1)} %collective-permute-done.6.refs_2_), channel_id=1, source_target_pairs={{0,2},{2,0},{4,6},{6,4},{8,10},{10,8},{12,14},{14,12},{16,30},{18,... | collective-permute-start | bytes 1966088 | tf_op jit(solution)/shard_map/ppermute | solution.py:59
  41.8 6.1 %shard_map.77.refs_4_ = f32[1024,128]{1,0:T(8,128)S(1)} custom-call(bf16[512,1024]{1,0:T(8,128)(2,1)S(1)} %bitcast.38, bf16[512,1024]{1,0:T(8,128)(2,1)S(1)} %collective-permute-done.5.sens_theirs, bf16[320,1024]{1,0:T(8,128)(2,1)S(1)} %collective-permute-done.refs_0_, bf16[320,1024]{1,0:T(8,128)(2,1)S(1)} %copy-done.16, ...), custom_call_target="tpu_custom_call" | custom-call | tf_op jit(solution)/shard_map/pallas_call | solution.py:126
  47.9 2.5 %shard_map.78 = f32[1024,128]{1,0:T(8,128)S(1)} custom-call(bf16[512,1024]{1,0:T(8,128)(2,1)S(1)} %bitcast.39, bf16[512,1024]{1,0:T(8,128)(2,1)S(1)} %collective-permute-done.5.sens_theirs, bf16[320,1024]{1,0:T(8,128)(2,1)S(1)} %collective-permute-done.9.refs_0_, bf16[320,1024]{1,0:T(8,128)(2,1)S(1)} %collective-permute-done.10.refs_1_, ...), custom_call_target="tpu_custom_call" | custom-call | tf_op jit(solution)/shard_map/pallas_call | solution.py:126
  54.3 1.0 fusion.27
  55.4 1.0 fusion.31
  56.5 1.1 collective-permute-start.15
  58.0 1.0 fusion.26
  59.0 1.0 fusion.30
  60.1 7.1 %collective-permute-done.15 = bf16[320,1024]{1,0:T(8,128)(2,1)S(1)} collective-permute-done((bf16[320,1024]{1,0:T(8,128)(2,1)S(1)}, bf16[320,1024]{1,0:T(8,128)(2,1)S(1)}, u32[]{:S(2)}, u32[]{:S(2)}) %collective-permute-start.15) | collective-permute-done | bytes 655392 | tf_op jit(solution)/shard_map/ppermute | solution.py:59
  67.2 1.4 %collective-permute-done.14 = bf16[320,1024]{1,0:T(8,128)(2,1)S(1)} collective-permute-done((bf16[320,1024]{1,0:T(8,128)(2,1)S(1)}, bf16[320,1024]{1,0:T(8,128)(2,1)S(1)}, u32[]{:S(2)}, u32[]{:S(2)}) %collective-permute-start.14) | collective-permute-done | bytes 655392 | tf_op jit(solution)/shard_map/ppermute | solution.py:68
  69.2 1.4 %collective-permute-start.16 = (bf16[320,1024]{1,0:T(8,128)(2,1)S(1)}, bf16[320,1024]{1,0:T(8,128)(2,1)S(1)}, u32[]{:S(2)}, u32[]{:S(2)}) collective-permute-start(bf16[320,1024]{1,0:T(8,128)(2,1)S(1)} %fusion.10), channel_id=1, source_target_pairs={{0,32},{16,112},{32,64},{48,16},{64,96},{80,48},{96,0},{112,80},{1... | collective-permute-start | bytes 1966088 | tf_op jit(solution)/shard_map/ppermute | solution.py:39
  72.6 1.0 fusion.33
  73.7 5.8 %collective-permute-done.17 = bf16[320,1024]{1,0:T(8,128)(2,1)S(1)} collective-permute-done((bf16[320,1024]{1,0:T(8,128)(2,1)S(1)}, bf16[320,1024]{1,0:T(8,128)(2,1)S(1)}, u32[]{:S(2)}, u32[]{:S(2)}) %collective-permute-start.17) | collective-permute-done | bytes 655392 | tf_op jit(solution)/shard_map/ppermute | solution.py:68
  79.5 1.6 %collective-permute-done.16 = bf16[320,1024]{1,0:T(8,128)(2,1)S(1)} collective-permute-done((bf16[320,1024]{1,0:T(8,128)(2,1)S(1)}, bf16[320,1024]{1,0:T(8,128)(2,1)S(1)}, u32[]{:S(2)}, u32[]{:S(2)}) %collective-permute-start.16) | collective-permute-done | bytes 655392 | tf_op jit(solution)/shard_map/ppermute | solution.py:39
  82.4 1.0 fusion.32
  83.4 8.3 %collective-permute-done.19 = bf16[320,1024]{1,0:T(8,128)(2,1)S(1)} collective-permute-done((bf16[320,1024]{1,0:T(8,128)(2,1)S(1)}, bf16[320,1024]{1,0:T(8,128)(2,1)S(1)}, u32[]{:S(2)}, u32[]{:S(2)}) %collective-permute-start.19) | collective-permute-done | bytes 655392 | tf_op jit(solution)/shard_map/ppermute | solution.py:68
  91.7 2.4 %collective-permute-done.20 = bf16[320,1024]{1,0:T(8,128)(2,1)S(1)} collective-permute-done((bf16[320,1024]{1,0:T(8,128)(2,1)S(1)}, bf16[320,1024]{1,0:T(8,128)(2,1)S(1)}, u32[]{:S(2)}, u32[]{:S(2)}) %collective-permute-start.20) | collective-permute-done | bytes 655392 | tf_op jit(solution)/shard_map/ppermute | solution.py:50
  94.4 23.3 %all_to_all.5 = bf16[8,320,128]{2,1,0:T(8,128)(2,1)S(1)} all-to-all(bf16[8,320,128]{2,1,0:T(8,128)(2,1)S(1)} %bitcast_bitcast_fusion), channel_id=1, replica_groups=mesh['fsdp'=16,'group'=8,'dp'=2] {'group'}, dimensions={0} | all-to-all | bytes 1310720 | tf_op jit(solution)/shard_map/all_to_all | solution.py:260
  117.8 2.2 %collective-permute-start.21 = (f32[320,128]{1,0:T(8,128)S(1)}, f32[320,128]{1,0:T(8,128)S(1)}, u32[]{:S(2)}, u32[]{:S(2)}) collective-permute-start(f32[320,128]{1,0:T(8,128)S(1)} %convert_reduce_fusion), channel_id=1, source_target_pairs={{0,1},{1,0},{2,3},{3,2},{4,5},{5,4},{6,7},{7,6},{8,9},{9,8},{10,11... | collective-permute-start | bytes 491528 | tf_op jit(solution)/shard_map/ppermute | solution.py:76
  120.0 4.7 %collective-permute-done.21 = f32[320,128]{1,0:T(8,128)S(1)} collective-permute-done((f32[320,128]{1,0:T(8,128)S(1)}, f32[320,128]{1,0:T(8,128)S(1)}, u32[]{:S(2)}, u32[]{:S(2)}) %collective-permute-start.21) | collective-permute-done | bytes 163872 | tf_op jit(solution)/shard_map/ppermute | solution.py:76
  (121 shorter events, 17.7 us)
Async XLA Ops:
  0.0 23.3 %collective-permute-start.4 = (bf16[512,5120]{1,0:T(8,128)(2,1)}, bf16[512,5120]{1,0:T(8,128)(2,1)}, u32[]{:S(2)}, u32[]{:S(2)}) collective-permute-start(bf16[512,5120]{1,0:T(8,128)(2,1)} %bitcast.41), channel_id=1, source_target_pairs={{0,16},{16,0},{32,48},{48,32},{64,80},{80,64},{96,112},{112,96},{1... | collective-permute-start | bytes 15728648 | tf_op jit(solution)/shard_map/ppermute | solution.py:34
  0.0 13.8 %collective-permute-start = (bf16[320,1024]{1,0:T(8,128)(2,1)}, bf16[320,1024]{1,0:T(8,128)(2,1)S(1)}, u32[]{:S(2)}, u32[]{:S(2)}) collective-permute-start(bf16[320,1024]{1,0:T(8,128)(2,1)} %refs_0_.1), channel_id=1, source_target_pairs={{32,0},{50,2},{36,4},{54,6},{40,8},{58,10},{44,12},{62,14},{112,16... | collective-permute-start | bytes 1966088 | tf_op jit(solution)/shard_map/ppermute | solution.py:50
  3.0 10.8 %collective-permute-start.1 = (bf16[320,1024]{1,0:T(8,128)(2,1)}, bf16[320,1024]{1,0:T(8,128)(2,1)S(1)}, u32[]{:S(2)}, u32[]{:S(2)}) collective-permute-start(bf16[320,1024]{1,0:T(8,128)(2,1)} %refs_0_.1), channel_id=1, source_target_pairs={{0,129},{1,128},{16,144},{17,145},{32,161},{33,160},{48,176},{49,1... | collective-permute-start | bytes 1966088 | tf_op jit(solution)/shard_map/ppermute | solution.py:68
  5.1 3.7 %collective-permute-start.2 = (f32[2,2,256]{2,1,0:T(2,128)S(1)}, f32[2,2,256]{2,1,0:T(2,128)S(1)}, u32[]{:S(2)}, u32[]{:S(2)}) collective-permute-start(f32[2,2,256]{2,1,0:T(2,128)S(1)} %broadcast_in_dim.2), channel_id=1, source_target_pairs={{0,2},{2,0},{4,6},{6,4},{8,10},{10,8},{12,14},{14,12},{1,3},{3,1},... | collective-permute-start | bytes 12296 | tf_op jit(solution)/shard_map/ppermute | solution.py:72
  5.7 26.2 %collective-permute-start.5 = (bf16[512,1024]{1,0:T(8,128)(2,1)}, bf16[512,1024]{1,0:T(8,128)(2,1)S(1)}, u32[]{:S(2)}, u32[]{:S(2)}) collective-permute-start(bf16[512,1024]{1,0:T(8,128)(2,1)} %bitcast.36), channel_id=1, source_target_pairs={{0,16},{16,0},{32,48},{48,32},{64,80},{80,64},{96,112},{112,96},{1... | collective-permute-start | bytes 3145736 | tf_op jit(solution)/shard_map/ppermute | solution.py:34
  8.8 4.9 %collective-permute-start.3 = (f32[2,2,256]{2,1,0:T(2,128)S(1)}, f32[2,2,256]{2,1,0:T(2,128)S(1)}, u32[]{:S(2)}, u32[]{:S(2)}) collective-permute-start(f32[2,2,256]{2,1,0:T(2,128)S(1)} %broadcast_add_fusion), channel_id=1, source_target_pairs={{0,4},{2,6},{4,0},{6,2},{8,12},{10,14},{12,8},{14,10},{1,5},{3,7},... | collective-permute-start | bytes 12296 | tf_op jit(solution)/shard_map/ppermute | solution.py:72
  13.8 9.5 %copy-start.29 = (f32[1,2,256]{2,1,0:T(2,128)S(1)}, f32[1,2,256]{2,1,0:T(2,128)}, u32[]{:S(2)}) copy-start(f32[1,2,256]{2,1,0:T(2,128)} %param.10) | copy-start | bytes 6148
  13.8 9.5 %copy-start.30 = (s32[1,2]{1,0:T(1,128)S(1)}, s32[1,2]{1,0:T(1,128)}, u32[]{:S(2)}) copy-start(s32[1,2]{1,0:T(1,128)} %param.12) | copy-start | bytes 28
  14.7 19.7 %collective-permute-start.6 = (bf16[320,1024]{1,0:T(8,128)(2,1)S(1)}, bf16[320,1024]{1,0:T(8,128)(2,1)}, u32[]{:S(2)}, u32[]{:S(2)}) collective-permute-start(bf16[320,1024]{1,0:T(8,128)(2,1)S(1)} %collective-permute-done.refs_0_), channel_id=1, source_target_pairs={{0,129},{1,128},{16,144},{17,145},{32,161},{33,160},{48,176},{49,1... | collective-permute-start | bytes 1966088 | tf_op jit(solution)/shard_map/ppermute | solution.py:68
  17.3 17.1 %collective-permute-start.7 = (bf16[320,1024]{1,0:T(8,128)(2,1)S(1)}, bf16[320,1024]{1,0:T(8,128)(2,1)}, u32[]{:S(2)}, u32[]{:S(2)}) collective-permute-start(bf16[320,1024]{1,0:T(8,128)(2,1)S(1)} %collective-permute-done.refs_0_), channel_id=1, source_target_pairs={{0,96},{16,48},{32,0},{48,80},{64,32},{80,112},{96,64},{112,16},{1... | collective-permute-start | bytes 1966088 | tf_op jit(solution)/shard_map/ppermute | solution.py:39
  18.1 16.3 %collective-permute-start.8 = (bf16[320,1024]{1,0:T(8,128)(2,1)S(1)}, bf16[320,1024]{1,0:T(8,128)(2,1)S(1)}, u32[]{:S(2)}, u32[]{:S(2)}) collective-permute-start(bf16[320,1024]{1,0:T(8,128)(2,1)S(1)} %collective-permute-done.refs_0_), channel_id=1, source_target_pairs={{0,2},{2,0},{4,6},{6,4},{8,10},{10,8},{12,14},{14,12},{16,30},{18,... | collective-permute-start | bytes 1966088 | tf_op jit(solution)/shard_map/ppermute | solution.py:59
  25.6 6.3 %copy-start = (bf16[1,2,256,1024]{3,2,1,0:T(8,128)(2,1)S(1)}, bf16[1,2,256,1024]{3,2,1,0:T(8,128)(2,1)}, u32[]{:S(2)}) copy-start(bf16[1,2,256,1024]{3,2,1,0:T(8,128)(2,1)} %param.9) | copy-start | bytes 3145732
  25.8 8.6 %copy-start.1 = (bf16[1024,384]{1,0:T(8,128)(2,1)}, bf16[1024,384]{1,0:T(8,128)(2,1)S(1)}, u32[]{:S(2)}) copy-start(bf16[1024,384]{1,0:T(8,128)(2,1)S(1)} %get-tuple-element.34.refs_3_) | copy-start | bytes 2359300
  25.8 8.6 %copy-start.13 = (bf16[1024,384]{1,0:T(8,128)(2,1)}, bf16[1024,384]{1,0:T(8,128)(2,1)S(1)}, u32[]{:S(2)}) copy-start(bf16[1024,384]{1,0:T(8,128)(2,1)S(1)} %get-tuple-element.31.refs_2_) | copy-start | bytes 2359300
  25.8 15.0 %collective-permute-start.11 = (f32[2,2,256]{2,1,0:T(2,128)S(1)}, f32[2,2,256]{2,1,0:T(2,128)S(1)}, u32[]{:S(2)}, u32[]{:S(2)}) collective-permute-start(f32[2,2,256]{2,1,0:T(2,128)S(1)} %fusion.50), channel_id=1, source_target_pairs={{0,8},{2,10},{4,12},{6,14},{8,0},{10,2},{12,4},{14,6},{1,9},{3,11}... | collective-permute-start | bytes 12296 | tf_op jit(solution)/shard_map/ppermute | solution.py:72
  31.9 6.3 %copy-start.24 = (bf16[512,384]{1,0:T(8,128)(2,1)S(1)}, bf16[512,384]{1,0:T(8,128)(2,1)}, u32[]{:S(2)}) copy-start(bf16[512,384]{1,0:T(8,128)(2,1)} %get-tuple-element.54) | copy-start | bytes 1179652
  31.9 6.2 %copy-start.25 = (bf16[512,384]{1,0:T(8,128)(2,1)S(1)}, bf16[512,384]{1,0:T(8,128)(2,1)}, u32[]{:S(2)}) copy-start(bf16[512,384]{1,0:T(8,128)(2,1)} %get-tuple-element.55) | copy-start | bytes 1179652
  34.4 13.4 %collective-permute-start.10 = (bf16[320,1024]{1,0:T(8,128)(2,1)}, bf16[320,1024]{1,0:T(8,128)(2,1)S(1)}, u32[]{:S(2)}, u32[]{:S(2)}) collective-permute-start(bf16[320,1024]{1,0:T(8,128)(2,1)} %collective-permute-done.7.refs_3_), channel_id=1, source_target_pairs={{0,129},{1,128},{16,144},{17,145},{32,161},{33,160},{48,176},{49,1... | collective-permute-start | bytes 1966088 | tf_op jit(solution)/shard_map/ppermute | solution.py:68
  36.7 11.1 %collective-permute-start.9 = (bf16[320,1024]{1,0:T(8,128)(2,1)}, bf16[320,1024]{1,0:T(8,128)(2,1)S(1)}, u32[]{:S(2)}, u32[]{:S(2)}) collective-permute-start(bf16[320,1024]{1,0:T(8,128)(2,1)} %collective-permute-done.6.refs_2_), channel_id=1, source_target_pairs={{0,2},{2,0},{4,6},{6,4},{8,10},{10,8},{12,14},{14,12},{16,30},{18,... | collective-permute-start | bytes 1966088 | tf_op jit(solution)/shard_map/ppermute | solution.py:59
  40.8 7.1 %copy-start.9 = (bf16[1024,384]{1,0:T(8,128)(2,1)}, bf16[1024,384]{1,0:T(8,128)(2,1)S(1)}, u32[]{:S(2)}) copy-start(bf16[1024,384]{1,0:T(8,128)(2,1)S(1)} %get-tuple-element.38.refs_3_) | copy-start | bytes 2359300
  40.8 7.1 %copy-start.11 = (bf16[1024,384]{1,0:T(8,128)(2,1)}, bf16[1024,384]{1,0:T(8,128)(2,1)S(1)}, u32[]{:S(2)}) copy-start(bf16[1024,384]{1,0:T(8,128)(2,1)S(1)} %get-tuple-element.37.refs_2_) | copy-start | bytes 2359300
  50.6 1.3 collective-permute-start.12
  50.7 1.3 %collective-permute-start.13 = (f32[1024]{0:T(1024)S(1)}, f32[1024]{0:T(1024)S(1)}, u32[]{:S(2)}, u32[]{:S(2)}) collective-permute-start(f32[1024]{0:T(1024)S(1)} %reduce_sum.28), channel_id=1, source_target_pairs={{0,16},{16,0},{32,48},{48,32},{64,80},{80,64},{96,112},{112,96},{1... | collective-permute-start | bytes 12296 | tf_op jit(solution)/shard_map/ppermute | solution.py:34
  56.5 10.7 %collective-permute-start.15 = (bf16[320,1024]{1,0:T(8,128)(2,1)S(1)}, bf16[320,1024]{1,0:T(8,128)(2,1)S(1)}, u32[]{:S(2)}, u32[]{:S(2)}) collective-permute-start(bf16[320,1024]{1,0:T(8,128)(2,1)S(1)} %fusion.12), channel_id=1, source_target_pairs={{0,2},{2,0},{4,6},{6,4},{8,10},{10,8},{12,14},{14,12},{16,30},{18,... | collective-permute-start | bytes 1966088 | tf_op jit(solution)/shard_map/ppermute | solution.py:59
  57.7 10.9 %collective-permute-start.14 = (bf16[320,1024]{1,0:T(8,128)(2,1)S(1)}, bf16[320,1024]{1,0:T(8,128)(2,1)S(1)}, u32[]{:S(2)}, u32[]{:S(2)}) collective-permute-start(bf16[320,1024]{1,0:T(8,128)(2,1)S(1)} %fusion.13), channel_id=1, source_target_pairs={{0,128},{1,129},{16,145},{17,144},{32,160},{33,161},{48,177},{49,1... | collective-permute-start | bytes 1966088 | tf_op jit(solution)/shard_map/ppermute | solution.py:68
  68.8 10.7 %collective-permute-start.17 = (bf16[320,1024]{1,0:T(8,128)(2,1)S(1)}, bf16[320,1024]{1,0:T(8,128)(2,1)S(1)}, u32[]{:S(2)}, u32[]{:S(2)}) collective-permute-start(bf16[320,1024]{1,0:T(8,128)(2,1)S(1)} %fusion.8), channel_id=1, source_target_pairs={{0,128},{1,129},{16,145},{17,144},{32,160},{33,161},{48,177},{49,1... | collective-permute-start | bytes 1966088 | tf_op jit(solution)/shard_map/ppermute | solution.py:68
  69.2 11.9 %collective-permute-start.16 = (bf16[320,1024]{1,0:T(8,128)(2,1)S(1)}, bf16[320,1024]{1,0:T(8,128)(2,1)S(1)}, u32[]{:S(2)}, u32[]{:S(2)}) collective-permute-start(bf16[320,1024]{1,0:T(8,128)(2,1)S(1)} %fusion.10), channel_id=1, source_target_pairs={{0,32},{16,112},{32,64},{48,16},{64,96},{80,48},{96,0},{112,80},{1... | collective-permute-start | bytes 1966088 | tf_op jit(solution)/shard_map/ppermute | solution.py:39
  70.5 10.6 %collective-permute-start.18 = (bf16[320,1024]{1,0:T(8,128)(2,1)S(1)}, bf16[320,1024]{1,0:T(8,128)(2,1)S(1)}, u32[]{:S(2)}, u32[]{:S(2)}) collective-permute-start(bf16[320,1024]{1,0:T(8,128)(2,1)S(1)} %fusion.14), channel_id=1, source_target_pairs={{0,2},{2,0},{4,6},{6,4},{8,10},{10,8},{12,14},{14,12},{16,30},{18,... | collective-permute-start | bytes 1966088 | tf_op jit(solution)/shard_map/ppermute | solution.py:59
  73.6 8.8 %copy-start.14 = (bf16[1024,384]{1,0:T(8,128)(2,1)S(1)}, bf16[1024,384]{1,0:T(8,128)(2,1)}, u32[]{:S(2)}) copy-start(bf16[1024,384]{1,0:T(8,128)(2,1)} %copy-done.13) | copy-start | bytes 2359300
  81.1 10.6 %collective-permute-start.19 = (bf16[320,1024]{1,0:T(8,128)(2,1)S(1)}, bf16[320,1024]{1,0:T(8,128)(2,1)S(1)}, u32[]{:S(2)}, u32[]{:S(2)}) collective-permute-start(bf16[320,1024]{1,0:T(8,128)(2,1)S(1)} %fusion.11), channel_id=1, source_target_pairs={{0,128},{1,129},{16,145},{17,144},{32,160},{33,161},{48,177},{49,1... | collective-permute-start | bytes 1966088 | tf_op jit(solution)/shard_map/ppermute | solution.py:68
  82.3 11.9 %collective-permute-start.20 = (bf16[320,1024]{1,0:T(8,128)(2,1)S(1)}, bf16[320,1024]{1,0:T(8,128)(2,1)S(1)}, u32[]{:S(2)}, u32[]{:S(2)}) collective-permute-start(bf16[320,1024]{1,0:T(8,128)(2,1)S(1)} %fusion.3), channel_id=1, source_target_pairs={{0,32},{2,50},{4,36},{6,54},{8,40},{10,58},{12,44},{14,62},{16,112... | collective-permute-start | bytes 1966088 | tf_op jit(solution)/shard_map/ppermute | solution.py:50
  117.8 6.9 %collective-permute-start.21 = (f32[320,128]{1,0:T(8,128)S(1)}, f32[320,128]{1,0:T(8,128)S(1)}, u32[]{:S(2)}, u32[]{:S(2)}) collective-permute-start(f32[320,128]{1,0:T(8,128)S(1)} %convert_reduce_fusion), channel_id=1, source_target_pairs={{0,1},{1,0},{2,3},{3,2},{4,5},{5,4},{6,7},{7,6},{8,9},{9,8},{10,11... | collective-permute-start | bytes 491528 | tf_op jit(solution)/shard_map/ppermute | solution.py:76
  (21 other events, 46.9 us)
